TPU v7x, 32 devices: a whole 2x2x4 slice. The times are simulated.
32 devices in a mesh: seq: 8 (over z, y), tp: 4 (over x, core).
Axes of the slice: x: 2, y: 2, z: 4, core: 2. Of those that a mesh axis runs over, the one named last changes fastest.
Arguments:
- subsampled: bfloat16 [2048, 4096], P('seq'), may hold values from -6 to 6
- proj_weight: bfloat16 [4096, 1024], P(None, 'tp'), may hold values from -0.09375 to 0.09375
- value_weight: bfloat16 [1024, 1024], P(None, 'tp'), may hold values from -0.1875 to 0.1875
- gate_weight: bfloat16 [1024, 1024], P(None, 'tp'), may hold values from -0.1875 to 0.1875
- conv_kernel: float32 [9, 1024], P(None, 'tp'), may hold values from -2 to 2
- bn_gain: float32 [1024], P('tp'), may hold values from 0.5 to 1.5
- bn_shift: float32 [1024], P('tp'), may hold values from -2 to 2
- down_weight: bfloat16 [1024, 1024], P(None, 'tp'), may hold values from -0.1875 to 0.1875
- clip_frames: int32 [8, 8], replicated, may hold values from 1 to 64, 256 in all within a row
- clip_dest: int32 [8, 8], replicated, may hold values from 0 to 7, each once within a row
- out_grad: bfloat16 [4096, 1024], P('seq', 'tp'), may hold values from -0.13183594 to 0.13183594
Outputs:
- block_out: bfloat16 [4096, 1024], P('seq', 'tp')
- proj_grad: float32 [4096, 1024], P('seq', 'tp')
- value_grad: float32 [1024, 1024], P('seq', 'tp')
- gate_grad: float32 [1024, 1024], P('seq', 'tp')
- down_grad: float32 [1024, 1024], P('seq', 'tp')
- bn_gain_grad: float32 [1024], P('tp')
- bn_shift_grad: float32 [1024], P('tp')
Inputs may be any that keep to these rules, and one draw needn't show every extreme that they name: `clip_frames`: row s holds the frame counts of the 8 clips of owner s, summing to 256; the largest of each row is 64. `clip_dest`: each row is a permutation: owner s sends exactly one clip to every packed shard.
All inputs are finite; a program needn't handle non-finite values.
Results may differ from a plain program's by a relative error of at most 0.0077.
Values may be sent and summed in bfloat16 or wider, within the bound.
A program may use at most 192 MiB of HBM per device.

v0:
```python
import jax
import jax.numpy as jnp
from jax import lax
from jax.sharding import PartitionSpec as P

MOST = 64


def depthwise(field, kernel):
    half = kernel.shape[0] // 2
    length = field.shape[1]
    padded = jnp.pad(field, ((0, 0), (half, half), (0, 0)))
    total = jnp.zeros(field.shape, jnp.float32)
    for offset in range(kernel.shape[0]):
        total = total + kernel[offset] * padded[:, offset : offset + length]
    return total


def depthwise_back(grad, kernel):
    half = kernel.shape[0] // 2
    length = grad.shape[1]
    padded = jnp.pad(grad, ((0, 0), (half, half), (0, 0)))
    total = jnp.zeros(grad.shape, jnp.float32)
    for offset in range(kernel.shape[0]):
        begin = 2 * half - offset
        total = total + kernel[offset] * padded[:, begin : begin + length]
    return total


def contract_rows(left, right):
    return lax.dot_general(
        left, right, (((0,), (0,)), ((), ())), preferred_element_type=jnp.float32
    )


def contract_cols(left, right):
    return lax.dot_general(
        left, right, (((1,), (1,)), ((), ())), preferred_element_type=jnp.float32
    )


def body(
    subsampled,
    proj_weight,
    value_weight,
    gate_weight,
    conv_kernel,
    bn_gain,
    bn_shift,
    down_weight,
    clip_frames,
    clip_dest,
    out_grad,
):
    shards = lax.axis_size("seq")
    seq_index = lax.axis_index("seq")
    tp_index = lax.axis_index("tp")
    own_rows = subsampled.shape[0]
    part_width = proj_weight.shape[1]
    count = float(own_rows * shards)
    clip_lens = lax.dynamic_slice_in_dim(clip_frames, seq_index, 1, 0)[0]
    clip_targets = lax.dynamic_slice_in_dim(clip_dest, seq_index, 1, 0)[0]
    offsets = jnp.cumsum(clip_lens) - clip_lens
    shard_ids = jnp.arange(shards, dtype=jnp.int32)
    match = clip_targets[None, :] == shard_ids[:, None]
    starts = jnp.sum(jnp.where(match, offsets[None, :], 0), axis=1)
    lengths = jnp.sum(jnp.where(match, clip_lens[None, :], 0), axis=1)
    frame_pos = jnp.arange(MOST, dtype=jnp.int32)
    source_rows = jnp.minimum(starts[:, None] + frame_pos[None, :], own_rows - 1).reshape(-1)
    send_valid = (frame_pos[None, :] < lengths[:, None]).reshape(-1, 1)
    projected = jnp.dot(subsampled, proj_weight, preferred_element_type=jnp.float32).astype(
        jnp.bfloat16
    )
    outgoing = jnp.where(
        send_valid, jnp.take(projected, source_rows, axis=0), jnp.zeros((), jnp.bfloat16)
    )
    arrived = lax.all_to_all(
        outgoing.reshape(shards, MOST, part_width), "seq", split_axis=0, concat_axis=0, tiled=True
    )
    hidden_part = arrived.reshape(shards * MOST, part_width)
    hidden_full = lax.all_gather(hidden_part, "tp", axis=1, tiled=True)
    incoming = clip_dest == seq_index
    in_lengths = jnp.sum(jnp.where(incoming, clip_frames, 0), axis=1)
    valid = (frame_pos[None, :] < in_lengths[:, None]).reshape(-1, 1)
    mask = valid.astype(jnp.float32)
    hidden32 = hidden_full.astype(jnp.float32)
    centred = hidden32 - jnp.mean(hidden32, axis=1, keepdims=True)
    sigma = jnp.sqrt(jnp.mean(centred * centred, axis=1, keepdims=True) + 1e-05)
    normed = centred / sigma
    normed16 = normed.astype(jnp.bfloat16)
    value_pre = jnp.dot(normed16, value_weight, preferred_element_type=jnp.float32)
    gate_pre = jnp.dot(normed16, gate_weight, preferred_element_type=jnp.float32)
    gate_sig = jax.nn.sigmoid(gate_pre)
    glu = value_pre * gate_sig * mask
    conv = depthwise(glu.reshape(shards, MOST, part_width), conv_kernel).reshape(-1, part_width)
    conv_total, square_total = lax.psum(
        (jnp.sum(conv * mask, axis=0), jnp.sum(conv * conv * mask, axis=0)), "seq"
    )
    conv_mean = conv_total / count
    conv_var = square_total / count - conv_mean * conv_mean
    bn_scale = jnp.sqrt(conv_var + 1e-05)
    bn_hat = (conv - conv_mean) / bn_scale
    batch_normed = bn_gain * bn_hat + bn_shift
    bn_sig = jax.nn.sigmoid(batch_normed)
    swish = (batch_normed * bn_sig).astype(jnp.bfloat16)
    mixed = lax.psum_scatter(
        contract_cols(swish, down_weight), "tp", scatter_dimension=1, tiled=True
    )
    block_out = ((hidden_part.astype(jnp.float32) + mixed) * mask).astype(jnp.bfloat16)
    grad_out = jnp.where(valid, out_grad, jnp.zeros((), jnp.bfloat16))
    grad_full = lax.all_gather(grad_out, "tp", axis=1, tiled=True)
    down_local = contract_rows(grad_full, swish)
    grad_swish = jnp.dot(grad_full, down_weight, preferred_element_type=jnp.float32)
    grad_bn = grad_swish * bn_sig * (1.0 + batch_normed * (1.0 - bn_sig)) * mask
    bn_shift_grad, bn_gain_grad = lax.psum(
        (jnp.sum(grad_bn, axis=0), jnp.sum(grad_bn * bn_hat, axis=0)), "seq"
    )
    grad_conv = (
        bn_gain / bn_scale * (grad_bn - (bn_shift_grad + bn_hat * bn_gain_grad) / count) * mask
    )
    grad_glu = (
        depthwise_back(grad_conv.reshape(shards, MOST, part_width), conv_kernel).reshape(
            -1, part_width
        )
        * mask
    )
    grad_value = (grad_glu * gate_sig).astype(jnp.bfloat16)
    grad_gate = (grad_glu * value_pre * gate_sig * (1.0 - gate_sig)).astype(jnp.bfloat16)
    value_local = contract_rows(normed16, grad_value)
    gate_local = contract_rows(normed16, grad_gate)
    normed_terms = contract_cols(grad_value, value_weight) + contract_cols(grad_gate, gate_weight)
    grad_normed = lax.psum(normed_terms, "tp")
    grad_hidden = (
        grad_normed
        - jnp.mean(grad_normed, axis=1, keepdims=True)
        - normed * jnp.mean(grad_normed * normed, axis=1, keepdims=True)
    ) / sigma
    grad_hidden = lax.dynamic_slice_in_dim(grad_hidden, tp_index * part_width, part_width, 1)
    grad_packed = ((grad_out.astype(jnp.float32) + grad_hidden) * mask).astype(jnp.bfloat16)
    returned = lax.all_to_all(
        grad_packed.reshape(shards, MOST, part_width),
        "seq",
        split_axis=0,
        concat_axis=0,
        tiled=True,
    )
    row_ids = jnp.arange(own_rows, dtype=jnp.int32)
    clip_ends = jnp.cumsum(clip_lens)
    clip_of_row = jnp.sum((clip_ends[None, :] <= row_ids[:, None]).astype(jnp.int32), axis=1)
    row_match = clip_of_row[:, None] == shard_ids[None, :]
    row_start = jnp.sum(jnp.where(row_match, offsets[None, :], 0), axis=1)
    row_target = jnp.sum(jnp.where(row_match, clip_targets[None, :], 0), axis=1)
    positions = row_target * MOST + row_ids - row_start
    grad_proj = jnp.take(returned.reshape(shards * MOST, part_width), positions, axis=0)
    proj_local = contract_rows(subsampled, grad_proj)
    proj_grad, value_grad, gate_grad, down_grad = (
        lax.psum_scatter(proj_local, "seq", scatter_dimension=0, tiled=True),
        lax.psum_scatter(value_local, "seq", scatter_dimension=0, tiled=True),
        lax.psum_scatter(gate_local, "seq", scatter_dimension=0, tiled=True),
        lax.psum_scatter(down_local, "seq", scatter_dimension=0, tiled=True),
    )
    return (block_out, proj_grad, value_grad, gate_grad, down_grad, bn_gain_grad, bn_shift_grad)


def solution(mesh):
    placed = (
        P("seq", None),
        P(None, "tp"),
        P(None, "tp"),
        P(None, "tp"),
        P(None, "tp"),
        P("tp"),
        P("tp"),
        P(None, "tp"),
        P(),
        P(),
        P("seq", "tp"),
    )
    return jax.shard_map(
        body,
        mesh=mesh,
        in_specs=placed,
        out_specs=(
            P("seq", "tp"),
            P("seq", "tp"),
            P("seq", "tp"),
            P("seq", "tp"),
            P("seq", "tp"),
            P("tp"),
            P("tp"),
        ),
        check_vma=False,
    )
```

profile of v0, /device:TPU:0, one launch (start us, length us, event | category | flops | bytes accessed | tf_op | source)
XLA Modules:
  0.0 502.0 jit_solution(10994392400143319582)
XLA Ops:
  7.2 0.8 fusion.52
  8.1 0.2 reduce-window.4
  8.2 0.7 fusion.50
  9.0 0.1 select_reduce_fusion.4
  9.5 2.3 convolution_convert_fusion
  11.8 2.0 gather_fusion
  13.8 0.2 select_select_fusion
  14.0 16.1 %all_to_all.10 = bf16[8,64,256]{2,1,0:T(8,128)(2,1)} all-to-all(bf16[8,64,256]{2,1,0:T(8,128)(2,1)S(1)} %select_select_fusion), channel_id=1, replica_groups=mesh['seq'=8,'tp'=4] {'seq'}, dimensions={0} | all-to-all | bytes 524288 | tf_op jit(solution)/shard_map/all_to_all | solution.py:77
  30.2 0.1 select_reduce_fusion.2
  30.4 0.1 lt.106
  30.5 0.8 broadcast_select_fusion
  31.4 14.7 %all-gather.3.cloned.1.call-done = bf16[512,1024]{1,0:T(8,128)(2,1)} async-done(((bf16[512,256]{1,0:T(8,128)(2,1)}), bf16[512,1024]{1,0:T(8,128)(2,1)}) %all-gather.3.cloned.1.call-update) | async-done | bytes 1048592 | tf_op jit(solution)/shard_map/all_gather | solution.py:81
  46.1 1.5 convert_reduce_fusion
  47.6 1.6 fusion.2
  49.3 1.7 fusion.61
  51.0 0.5 fusion.6
  51.5 0.8 copy-done.6
  52.2 1.2 multiply_multiply_fusion.1
  53.5 1.5 multiply_reduce_fusion.3
  55.0 21.3 %all-reduce.3 = (f32[256]{0:T(256)S(1)}, f32[256]{0:T(256)S(1)}) all-reduce(f32[256]{0:T(256)S(1)} %get-tuple-element.31, f32[256]{0:T(256)S(1)} %get-tuple-element.30), channel_id=1, replica_groups=mesh['seq'=8,'tp'=4] {'seq'}, use_global_device_ids=true, to_apply=%region_9.10 | all-reduce | flops 512 | bytes 4096 | tf_op jit(solution)/shard_map/psum | solution.py:96
  76.3 1.9 fusion.44
  78.2 2.8 fusion.58
  81.0 17.1 %all-reduce.2 = (f32[256]{0:T(256)S(1)}, f32[256]{0:T(256)S(1)}) all-reduce(f32[256]{0:T(256)S(1)} %get-tuple-element.33, f32[256]{0:T(256)S(1)} %get-tuple-element.32), channel_id=1, replica_groups=mesh['seq'=8,'tp'=4] {'seq'}, use_global_device_ids=true, to_apply=%region_17.18 | all-reduce | flops 512 | bytes 4096 | tf_op jit(solution)/shard_map/psum | solution.py:115
  98.2 1.5 multiply_multiply_fusion
  99.7 0.5 fusion.32
  100.3 0.2 multiply_convert_fusion
  100.5 0.7 copy-done.5
  101.2 0.5 fusion.64
  101.7 1.8 convolution_add_fusion
  103.6 3.0 fusion.56
  106.7 0.1 select_reduce_fusion.1
  106.8 46.0 %all-reduce.6.cloned.1.call-done = f32[512,1024]{1,0:T(8,128)} async-done(((f32[512,1024]{1,0:T(8,128)}), f32[512,1024]{1,0:T(8,128)}) %all-reduce.6.cloned.1.call-update) | async-done | bytes 2097168 | tf_op jit(solution)/shard_map/psum | solution.py:132
  152.8 2.6 fusion.57
  155.5 31.4 %reduce-scatter.6.cloned.1.call-done = f32[512,256]{1,0:T(8,128)} async-done(((f32[512,1024]{1,0:T(8,128)}), f32[512,256]{1,0:T(8,128)}) %reduce-scatter.6.cloned.1.call-update) | async-done | bytes 524304 | tf_op jit(solution)/shard_map/reduce_scatter | solution.py:106
  186.9 2.6 fusion.45
  189.5 5.5 %all-to-all-start.1 = ((bf16[8,64,256]{2,1,0:T(8,128)(2,1)}), bf16[8,64,256]{2,1,0:T(8,128)(2,1)S(1)}, u32[]{:S(2)}, u32[]{:S(2)}) async-start(bf16[8,64,256]{2,1,0:T(8,128)(2,1)} %bitcast.70), calls=%async_computation.2 | async-start | bytes 524288 | tf_op jit(solution)/shard_map/all_to_all | solution.py:140
  195.1 8.8 %all-to-all-done.1 = bf16[8,64,256]{2,1,0:T(8,128)(2,1)S(1)} async-done(((bf16[8,64,256]{2,1,0:T(8,128)(2,1)}), bf16[8,64,256]{2,1,0:T(8,128)(2,1)S(1)}, u32[]{:S(2)}, u32[]{:S(2)}) %all-to-all-start.1) | async-done | bytes 262176 | tf_op jit(solution)/shard_map/all_to_all | solution.py:140
  203.9 1.2 gather_fusion.1
  205.1 2.7 convolution_bitcast_fusion
  207.9 0.6 copy-done.21
  208.5 2.9 fusion.55
  211.5 2.4 fusion.65
  214.0 1.5 fusion.66
  215.5 79.0 %reduce-scatter.8.cloned.1.call-done = f32[512,256]{0,1:T(8,128)} async-done(((f32[4096,256]{0,1:T(8,128)}), f32[512,256]{0,1:T(8,128)}) %reduce-scatter.8.cloned.1.call-update) | async-done | bytes 524304 | tf_op jit(solution)/shard_map/reduce_scatter | solution.py:157
  294.6 2.0 copy.20
  296.6 65.3 %reduce-scatter.14.cloned.1.call-done = f32[128,256]{1,0:T(8,128)} async-done(((f32[1024,256]{1,0:T(8,128)}), f32[128,256]{1,0:T(8,128)}) %reduce-scatter.14.cloned.1.call-update) | async-done | bytes 131088 | tf_op jit(solution)/shard_map/reduce_scatter | solution.py:160
  361.9 66.5 %reduce-scatter.10.cloned.1.call-done = f32[128,256]{1,0:T(8,128)} async-done(((f32[1024,256]{1,0:T(8,128)}), f32[128,256]{1,0:T(8,128)}) %reduce-scatter.10.cloned.1.call-update) | async-done | bytes 131088 | tf_op jit(solution)/shard_map/reduce_scatter | solution.py:158
  428.4 66.8 %reduce-scatter.12.cloned.1.call-done = f32[128,256]{1,0:T(8,128)} async-done(((f32[1024,256]{1,0:T(8,128)}), f32[128,256]{1,0:T(8,128)}) %reduce-scatter.12.cloned.1.call-update) | async-done | bytes 131088 | tf_op jit(solution)/shard_map/reduce_scatter | solution.py:159
  (77 shorter events, 1.1 us)
Async XLA Ops:
  7.2 2.3 copy-start
  7.2 38.9 %all-gather.3.cloned.1.call-start = ((), (), s32[]{:S(2)}) async-start(), calls=%async_computation.7 | async-start | bytes 1310720 | tf_op jit(solution)/shard_map/all_gather | solution.py:81
  11.8 18.4 %copy-start.15 = (s32[8,8]{1,0:T(8,128)S(1)}, s32[8,8]{1,0:T(8,128)}, u32[]{:S(2)}) copy-start(s32[8,8]{1,0:T(8,128)} %param.19) | copy-start | bytes 772
  11.8 18.4 %copy-start.16 = (s32[8,8]{1,0:T(8,128)S(1)}, s32[8,8]{1,0:T(8,128)}, u32[]{:S(2)}) copy-start(s32[8,8]{1,0:T(8,128)} %param.20) | copy-start | bytes 772
  11.8 18.7 %copy-start.11 = (bf16[512,256]{1,0:T(8,128)(2,1)S(1)}, bf16[512,256]{1,0:T(8,128)(2,1)}, u32[]{:S(2)}) copy-start(bf16[512,256]{1,0:T(8,128)(2,1)} %param.21) | copy-start | bytes 786436
  11.8 19.6 %copy-start.14 = (f32[9,256]{1,0:T(8,128)S(1)}, f32[9,256]{1,0:T(8,128)}, u32[]{:S(2)}) copy-start(f32[9,256]{1,0:T(8,128)} %param.15) | copy-start | bytes 27652
  30.1 48.1 %all-gather.5.cloned.1.call-start = ((), (), s32[]{:S(2)}) async-start(), calls=%async_computation.9 | async-start | bytes 1310720 | tf_op jit(solution)/shard_map/all_gather | solution.py:111
  31.3 121.5 %all-reduce.6.cloned.1.call-start = ((), (), s32[]{:S(2)}) async-start(), calls=%async_computation.10 | async-start | bytes 4194304 | tf_op jit(solution)/shard_map/psum | solution.py:132
  46.1 3.2 copy-start.1
  49.3 1.7 copy-start.12
  51.0 1.3 copy-start.9
  51.4 0.8 copy-start.6
  52.2 24.1 %copy-start.17 = (f32[256]{0:T(256)S(1)}, f32[256]{0:T(256)}, u32[]{:S(2)}) copy-start(f32[256]{0:T(256)} %param.16) | copy-start | bytes 3076
  52.2 26.0 %copy-start.20 = (f32[256]{0:T(256)S(1)}, f32[256]{0:T(256)}, u32[]{:S(2)}) copy-start(f32[256]{0:T(256)} %param.17) | copy-start | bytes 3076
  98.2 2.3 copy-start.18
  98.2 2.3 copy-start.19
  98.2 2.1 copy-start.7
  98.2 2.1 copy-start.8
  98.2 3.0 copy-start.10
  100.2 1.4 copy-start.13
  100.5 0.7 copy-start.5
  100.5 1.2 copy-start.2
  103.5 83.4 %reduce-scatter.6.cloned.1.call-start = ((), (), s32[]{:S(2)}) async-start(), calls=%async_computation.8 | async-start | bytes 2621440 | tf_op jit(solution)/shard_map/reduce_scatter | solution.py:106
  152.8 34.1 %copy-start.4 = (bf16[8,64,256]{2,1,0:T(8,128)(2,1)S(1)}, bf16[8,64,256]{2,1,0:T(8,128)(2,1)}, u32[]{:S(2)}) copy-start(bf16[8,64,256]{2,1,0:T(8,128)(2,1)} %all_to_all.10) | copy-start | bytes 786436
  189.5 14.4 %all-to-all-start.1 = ((bf16[8,64,256]{2,1,0:T(8,128)(2,1)}), bf16[8,64,256]{2,1,0:T(8,128)(2,1)S(1)}, u32[]{:S(2)}, u32[]{:S(2)}) async-start(bf16[8,64,256]{2,1,0:T(8,128)(2,1)} %bitcast.70), calls=%async_computation.2 | async-start | bytes 524288 | tf_op jit(solution)/shard_map/all_to_all | solution.py:140
  195.0 99.5 %reduce-scatter.8.cloned.1.call-start = ((), (), s32[]{:S(2)}) async-start(), calls=%async_computation.11 | async-start | bytes 4718592 | tf_op jit(solution)/shard_map/reduce_scatter | solution.py:157
  207.8 0.7 copy-start.21
  207.9 154.0 %reduce-scatter.14.cloned.1.call-start = ((), (), s32[]{:S(2)}) async-start(), calls=%async_computation.14 | async-start | bytes 1179648 | tf_op jit(solution)/shard_map/reduce_scatter | solution.py:160
  211.4 2.6 copy-start.3
  211.5 216.9 %reduce-scatter.10.cloned.1.call-start = ((), (), s32[]{:S(2)}) async-start(), calls=%async_computation.12 | async-start | bytes 1179648 | tf_op jit(solution)/shard_map/reduce_scatter | solution.py:158
  214.0 281.2 %reduce-scatter.12.cloned.1.call-start = ((), (), s32[]{:S(2)}) async-start(), calls=%async_computation.13 | async-start | bytes 1179648 | tf_op jit(solution)/shard_map/reduce_scatter | solution.py:159
Sparse Core Ops, SparseCore 0:
  30.2 15.8 all-gather.2
  48.2 16.8 all-gather.4
  103.6 49.1 all-reduce.5
  155.4 31.4 reduce-scatter.5
  208.0 86.5 reduce-scatter.7
  298.8 63.0 reduce-scatter.13
  365.9 62.4 reduce-scatter.9
  432.7 62.3 reduce-scatter.11
where the time goes:
time: 503 us; the launch traced here: 502 us
  waiting for transfers between devices  379 us (75%)
  blocking collectives  54.6 us (11%)
  matrix products  21.7 us (4%)
  other arithmetic  18.4 us (4%)
  between operations  14.5 us (3%)
  local copies, waits for them, and re-layouts  8.33 us (2%)
  starting transfers between devices  5.84 us (1%)
    reduce_scatter x1, waiting for transfers between devices, body(): lax.psum_scatter(proj_local, 'seq', scatter_dimension=0, tiled=True)  79 us
    reduce_scatter x1, waiting for transfers between devices, body(): lax.psum_scatter(gate_local, 'seq', scatter_dimension=0, tiled=True)  66.8 us
    reduce_scatter x1, waiting for transfers between devices, body(): lax.psum_scatter(value_local, 'seq', scatter_dimension=0, tiled=True)  66.5 us
    reduce_scatter x1, waiting for transfers between devices, body(): lax.psum_scatter(down_local, 'seq', scatter_dimension=0, tiled=True)  65.3 us
    psum x1, waiting for transfers between devices, body(): grad_normed = lax.psum(normed_terms, 'tp')  46 us
    reduce_scatter x1, waiting for transfers between devices, body(): lax.psum_scatter(contract_cols(swish, down_weight), 'tp', scatter_dimensi...  31.4 us
    psum x1, blocking collectives, body(): lax.psum((jnp.sum(conv * mask, axis=0), jnp.sum(conv * conv * mask, axis=...  21.3 us
    psum x1, blocking collectives, body(): lax.psum((jnp.sum(grad_bn, axis=0), jnp.sum(grad_bn * bn_hat, axis=0)), '...  17.1 us
  transfers between devices with their start and end apart: 9, of which 8 were waited for; matrix products, arithmetic and copies ran while one was open for 5% of the time, Pallas kernels for 0%

commit v1 on v0

--- a/solution.py
+++ b/solution.py
@@ -2,8 +2,24 @@
 import jax.numpy as jnp
 from jax import lax
 from jax.sharding import PartitionSpec as P
+from jax.lax import axis_index, axis_size, ppermute
 
 MOST = 64
+
+
+def pack_sectors(block_here, pos_dim, in_dim):
+    ax_name = "seq"
+    parts_out, tall = (axis_size(ax_name), axis_index(ax_name))
+    small = block_here.shape[pos_dim] // parts_out
+    main = jnp.roll(block_here, -tall * small, pos_dim)
+    block_list = [lax.slice_in_dim(main, 0, small, axis=pos_dim)]
+    for dev_i in [*range(1, parts_out)]:
+        oldest = lax.slice_in_dim(main, dev_i * small, (dev_i + 1) * small, axis=pos_dim)
+        block_list.append(
+            ppermute(oldest, ax_name, [(w, (w + dev_i) % parts_out) for w in range(parts_out)])
+        )
+    local_next = jnp.concatenate(block_list[::-1], in_dim)
+    return jnp.roll(local_next, (tall + 1) * block_list[0].shape[in_dim], in_dim)
 
 
 def depthwise(field, kernel):
@@ -74,9 +90,7 @@
     outgoing = jnp.where(
         send_valid, jnp.take(projected, source_rows, axis=0), jnp.zeros((), jnp.bfloat16)
     )
-    arrived = lax.all_to_all(
-        outgoing.reshape(shards, MOST, part_width), "seq", split_axis=0, concat_axis=0, tiled=True
-    )
+    arrived = pack_sectors(outgoing.reshape(shards, MOST, part_width), 0, 0)
     hidden_part = arrived.reshape(shards * MOST, part_width)
     hidden_full = lax.all_gather(hidden_part, "tp", axis=1, tiled=True)
     incoming = clip_dest == seq_index

time: 503 us -> 512 us (1.018)
  blocking collectives: 54.6 us -> 38.5 us
  starting transfers between devices: 5.84 us -> 20.7 us
  waiting for transfers between devices: 379 us -> 388 us
    all_to_all x1 -> x0, blocking collectives: 16.1 us -> none  [body(): lax.all_to_all(outgoing.reshape(shards, MOST, part_width), 'seq', split_a...]
    ppermute x0 -> x7, starting transfers between devices: none -> 14.9 us  [pack_sectors(): ppermute(oldest, ax_name, [(w, (w + dev_i) % parts_out) for w in range(pa...]
    ppermute x0 -> x7, waiting for transfers between devices: none -> 5.78 us  [pack_sectors(): ppermute(oldest, ax_name, [(w, (w + dev_i) % parts_out) for w in range(pa...]
  transfers between devices with their start and end apart: 9 -> 16, of which waited for: 8 -> 10; matrix products, arithmetic and copies ran while one was open for 5% -> 5% of each run, Pallas kernels for 0% -> 0%
where the time goes in v1:
time: 512 us; the launch traced here: 511 us
  waiting for transfers between devices  388 us (76%)
  blocking collectives  38.5 us (8%)
  matrix products  21.7 us (4%)
  starting transfers between devices  20.7 us (4%)
  other arithmetic  19.3 us (4%)
  between operations  14.6 us (3%)
  local copies, waits for them, and re-layouts  8.39 us (2%)
    reduce_scatter x1, waiting for transfers between devices, body(): lax.psum_scatter(proj_local, 'seq', scatter_dimension=0, tiled=True)  79 us
    reduce_scatter x1, waiting for transfers between devices, body(): lax.psum_scatter(gate_local, 'seq', scatter_dimension=0, tiled=True)  66.9 us
    reduce_scatter x1, waiting for transfers between devices, body(): lax.psum_scatter(value_local, 'seq', scatter_dimension=0, tiled=True)  66.5 us
    reduce_scatter x1, waiting for transfers between devices, body(): lax.psum_scatter(down_local, 'seq', scatter_dimension=0, tiled=True)  65.4 us
    psum x1, waiting for transfers between devices, body(): grad_normed = lax.psum(normed_terms, 'tp')  46 us
    reduce_scatter x1, waiting for transfers between devices, body(): lax.psum_scatter(contract_cols(swish, down_weight), 'tp', scatter_dimensi...  31.4 us
    psum x1, blocking collectives, body(): lax.psum((jnp.sum(conv * mask, axis=0), jnp.sum(conv * conv * mask, axis=...  21.3 us
    all_gather x1, waiting for transfers between devices, body(): hidden_full = lax.all_gather(hidden_part, 'tp', axis=1, tiled=True)  18.3 us
  transfers between devices with their start and end apart: 16, of which 10 were waited for; matrix products, arithmetic and copies ran while one was open for 5% of the time, Pallas kernels for 0%

profile of v1, /device:TPU:0, one launch (start us, length us, event | category | flops | bytes accessed | tf_op | source)
XLA Modules:
  0.0 511.5 jit_solution(2045455336694640252)
XLA Ops:
  7.2 0.8 fusion.54
  8.3 0.7 fusion.52
  9.5 2.3 convolution_convert_fusion
  11.8 2.0 gather_fusion
  14.2 6.1 %collective-permute-start = (bf16[1,64,256]{2,1,0:T(8,128)(2,1)S(1)}, bf16[1,64,256]{2,1,0:T(8,128)(2,1)S(1)}, u32[]{:S(2)}, u32[]{:S(2)}) collective-permute-start(bf16[1,64,256]{2,1,0:T(8,128)(2,1)S(1)} %get-tuple-element.56), channel_id=1, source_target_pairs={{0,28},{4,0},{8,4},{12,8},{16,12},{20,16},{24,20},{28,24},{1,29},{... | collective-permute-start | bytes 98312 | tf_op jit(solution)/shard_map/ppermute | solution.py:19
  20.2 2.5 collective-permute-start.4
  22.7 2.8 collective-permute-start.3
  25.5 2.9 collective-permute-start.1
  28.4 1.6 collective-permute-done.1
  30.0 0.6 collective-permute-start.2
  30.7 4.2 collective-permute-done.2
  34.9 0.8 fusion.46
  36.1 0.8 broadcast_select_fusion
  37.1 18.3 %all-gather.3.cloned.1.call-done = bf16[512,1024]{1,0:T(8,128)(2,1)} async-done(((bf16[512,256]{1,0:T(8,128)(2,1)}), bf16[512,1024]{1,0:T(8,128)(2,1)}) %all-gather.3.cloned.1.call-update) | async-done | bytes 1048592 | tf_op jit(solution)/shard_map/all_gather | solution.py:95
  55.4 1.5 convert_reduce_fusion
  56.9 1.6 fusion.2
  58.6 1.7 fusion.63
  60.2 0.5 fusion.6
  60.7 0.8 copy-done.6
  61.5 1.2 multiply_multiply_fusion.1
  62.7 1.5 multiply_reduce_fusion.3
  64.2 21.3 %all-reduce.3 = (f32[256]{0:T(256)S(1)}, f32[256]{0:T(256)S(1)}) all-reduce(f32[256]{0:T(256)S(1)} %get-tuple-element.32, f32[256]{0:T(256)S(1)} %get-tuple-element.31), channel_id=1, replica_groups=mesh['seq'=8,'tp'=4] {'seq'}, use_global_device_ids=true, to_apply=%region_9.11 | all-reduce | flops 512 | bytes 4096 | tf_op jit(solution)/shard_map/psum | solution.py:110
  85.5 1.9 fusion.44
  87.4 2.8 fusion.60
  90.3 17.1 %all-reduce.2 = (f32[256]{0:T(256)S(1)}, f32[256]{0:T(256)S(1)}) all-reduce(f32[256]{0:T(256)S(1)} %get-tuple-element.34, f32[256]{0:T(256)S(1)} %get-tuple-element.33), channel_id=1, replica_groups=mesh['seq'=8,'tp'=4] {'seq'}, use_global_device_ids=true, to_apply=%region_17.19 | all-reduce | flops 512 | bytes 4096 | tf_op jit(solution)/shard_map/psum | solution.py:129
  107.4 1.5 multiply_multiply_fusion
  108.9 0.5 fusion.32
  109.7 0.7 copy-done.5
  110.4 0.5 fusion.67
  110.9 1.8 convolution_add_fusion
  112.8 3.0 fusion.58
  116.0 46.0 %all-reduce.6.cloned.1.call-done = f32[512,1024]{1,0:T(8,128)} async-done(((f32[512,1024]{1,0:T(8,128)}), f32[512,1024]{1,0:T(8,128)}) %all-reduce.6.cloned.1.call-update) | async-done | bytes 2097168 | tf_op jit(solution)/shard_map/psum | solution.py:146
  162.1 2.6 fusion.59
  164.7 31.4 %reduce-scatter.6.cloned.1.call-done = f32[512,256]{1,0:T(8,128)} async-done(((f32[512,1024]{1,0:T(8,128)}), f32[512,256]{1,0:T(8,128)}) %reduce-scatter.6.cloned.1.call-update) | async-done | bytes 524304 | tf_op jit(solution)/shard_map/reduce_scatter | solution.py:120
  196.1 2.6 fusion.45
  198.8 5.5 %all-to-all-start = ((bf16[8,64,256]{2,1,0:T(8,128)(2,1)}), bf16[8,64,256]{2,1,0:T(8,128)(2,1)S(1)}, u32[]{:S(2)}, u32[]{:S(2)}) async-start(bf16[8,64,256]{2,1,0:T(8,128)(2,1)} %bitcast.70), calls=%async_computation.1 | async-start | bytes 524288 | tf_op jit(solution)/shard_map/all_to_all | solution.py:154
  204.4 8.8 %all-to-all-done = bf16[8,64,256]{2,1,0:T(8,128)(2,1)S(1)} async-done(((bf16[8,64,256]{2,1,0:T(8,128)(2,1)}), bf16[8,64,256]{2,1,0:T(8,128)(2,1)S(1)}, u32[]{:S(2)}, u32[]{:S(2)}) %all-to-all-start) | async-done | bytes 262176 | tf_op jit(solution)/shard_map/all_to_all | solution.py:154
  213.2 1.2 gather_fusion.1
  214.3 2.8 convolution_bitcast_fusion
  217.2 0.6 copy-done.21
  217.8 2.9 fusion.57
  220.8 2.4 fusion.68
  223.3 1.5 fusion.69
  224.8 79.0 %reduce-scatter.8.cloned.1.call-done = f32[512,256]{0,1:T(8,128)} async-done(((f32[4096,256]{0,1:T(8,128)}), f32[512,256]{0,1:T(8,128)}) %reduce-scatter.8.cloned.1.call-update) | async-done | bytes 524304 | tf_op jit(solution)/shard_map/reduce_scatter | solution.py:171
  303.8 2.0 copy.20
  305.8 65.4 %reduce-scatter.14.cloned.1.call-done = f32[128,256]{1,0:T(8,128)} async-done(((f32[1024,256]{1,0:T(8,128)}), f32[128,256]{1,0:T(8,128)}) %reduce-scatter.14.cloned.1.call-update) | async-done | bytes 131088 | tf_op jit(solution)/shard_map/reduce_scatter | solution.py:174
  371.2 66.5 %reduce-scatter.10.cloned.1.call-done = f32[128,256]{1,0:T(8,128)} async-done(((f32[1024,256]{1,0:T(8,128)}), f32[128,256]{1,0:T(8,128)}) %reduce-scatter.10.cloned.1.call-update) | async-done | bytes 131088 | tf_op jit(solution)/shard_map/reduce_scatter | solution.py:172
  437.7 66.9 %reduce-scatter.12.cloned.1.call-done = f32[128,256]{1,0:T(8,128)} async-done(((f32[1024,256]{1,0:T(8,128)}), f32[128,256]{1,0:T(8,128)}) %reduce-scatter.12.cloned.1.call-update) | async-done | bytes 131088 | tf_op jit(solution)/shard_map/reduce_scatter | solution.py:173
  (101 shorter events, 2.3 us)
Async XLA Ops:
  7.2 2.3 copy-start
  7.2 48.2 %all-gather.3.cloned.1.call-start = ((), (), s32[]{:S(2)}) async-start(), calls=%async_computation.6 | async-start | bytes 1310720 | tf_op jit(solution)/shard_map/all_gather | solution.py:95
  11.8 24.0 %copy-start.15 = (s32[8,8]{1,0:T(8,128)S(1)}, s32[8,8]{1,0:T(8,128)}, u32[]{:S(2)}) copy-start(s32[8,8]{1,0:T(8,128)} %param.21) | copy-start | bytes 772
  11.8 24.0 %copy-start.16 = (s32[8,8]{1,0:T(8,128)S(1)}, s32[8,8]{1,0:T(8,128)}, u32[]{:S(2)}) copy-start(s32[8,8]{1,0:T(8,128)} %param.22) | copy-start | bytes 772
  11.8 24.3 %copy-start.11 = (bf16[512,256]{1,0:T(8,128)(2,1)S(1)}, bf16[512,256]{1,0:T(8,128)(2,1)}, u32[]{:S(2)}) copy-start(bf16[512,256]{1,0:T(8,128)(2,1)} %param.23) | copy-start | bytes 786436
  13.8 23.3 %copy-start.14 = (f32[9,256]{1,0:T(8,128)S(1)}, f32[9,256]{1,0:T(8,128)}, u32[]{:S(2)}) copy-start(f32[9,256]{1,0:T(8,128)} %param.17) | copy-start | bytes 27652
  14.2 11.4 %collective-permute-start = (bf16[1,64,256]{2,1,0:T(8,128)(2,1)S(1)}, bf16[1,64,256]{2,1,0:T(8,128)(2,1)S(1)}, u32[]{:S(2)}, u32[]{:S(2)}) collective-permute-start(bf16[1,64,256]{2,1,0:T(8,128)(2,1)S(1)} %get-tuple-element.56), channel_id=1, source_target_pairs={{0,28},{4,0},{8,4},{12,8},{16,12},{20,16},{24,20},{28,24},{1,29},{... | collective-permute-start | bytes 98312 | tf_op jit(solution)/shard_map/ppermute | solution.py:19
  20.2 14.7 %collective-permute-start.6 = (bf16[1,64,256]{2,1,0:T(8,128)(2,1)S(1)}, bf16[1,64,256]{2,1,0:T(8,128)(2,1)S(1)}, u32[]{:S(2)}, u32[]{:S(2)}) collective-permute-start(bf16[1,64,256]{2,1,0:T(8,128)(2,1)S(1)} %get-tuple-element.50), channel_id=1, source_target_pairs={{0,4},{4,8},{8,12},{12,16},{16,20},{20,24},{24,28},{28,0},{1,5},{5... | collective-permute-start | bytes 98312 | tf_op jit(solution)/shard_map/ppermute | solution.py:19
  20.2 14.7 %collective-permute-start.5 = (bf16[1,64,256]{2,1,0:T(8,128)(2,1)S(1)}, bf16[1,64,256]{2,1,0:T(8,128)(2,1)S(1)}, u32[]{:S(2)}, u32[]{:S(2)}) collective-permute-start(bf16[1,64,256]{2,1,0:T(8,128)(2,1)S(1)} %get-tuple-element.51), channel_id=1, source_target_pairs={{0,8},{4,12},{8,16},{12,20},{16,24},{20,28},{24,0},{28,4},{1,9},{5... | collective-permute-start | bytes 98312 | tf_op jit(solution)/shard_map/ppermute | solution.py:19
  20.2 14.6 %collective-permute-start.4 = (bf16[1,64,256]{2,1,0:T(8,128)(2,1)S(1)}, bf16[1,64,256]{2,1,0:T(8,128)(2,1)S(1)}, u32[]{:S(2)}, u32[]{:S(2)}) collective-permute-start(bf16[1,64,256]{2,1,0:T(8,128)(2,1)S(1)} %get-tuple-element.52), channel_id=1, source_target_pairs={{0,12},{4,16},{8,20},{12,24},{16,28},{20,0},{24,4},{28,8},{1,13},{... | collective-permute-start | bytes 98312 | tf_op jit(solution)/shard_map/ppermute | solution.py:19
  22.7 12.2 %collective-permute-start.3 = (bf16[1,64,256]{2,1,0:T(8,128)(2,1)S(1)}, bf16[1,64,256]{2,1,0:T(8,128)(2,1)S(1)}, u32[]{:S(2)}, u32[]{:S(2)}) collective-permute-start(bf16[1,64,256]{2,1,0:T(8,128)(2,1)S(1)} %get-tuple-element.53), channel_id=1, source_target_pairs={{0,16},{4,20},{8,24},{12,28},{16,0},{20,4},{24,8},{28,12},{1,17},{... | collective-permute-start | bytes 98312 | tf_op jit(solution)/shard_map/ppermute | solution.py:19
  25.5 4.5 collective-permute-start.1
  30.0 4.8 collective-permute-start.2
  35.8 51.7 %all-gather.5.cloned.1.call-start = ((), (), s32[]{:S(2)}) async-start(), calls=%async_computation.8 | async-start | bytes 1310720 | tf_op jit(solution)/shard_map/all_gather | solution.py:125
  37.0 125.1 %all-reduce.6.cloned.1.call-start = ((), (), s32[]{:S(2)}) async-start(), calls=%async_computation.9 | async-start | bytes 4194304 | tf_op jit(solution)/shard_map/psum | solution.py:146
  55.4 3.2 copy-start.1
  58.6 1.7 copy-start.12
  60.2 1.3 copy-start.9
  60.7 0.8 copy-start.6
  61.5 24.0 %copy-start.17 = (f32[256]{0:T(256)S(1)}, f32[256]{0:T(256)}, u32[]{:S(2)}) copy-start(f32[256]{0:T(256)} %param.18) | copy-start | bytes 3076
  61.5 25.9 %copy-start.20 = (f32[256]{0:T(256)S(1)}, f32[256]{0:T(256)}, u32[]{:S(2)}) copy-start(f32[256]{0:T(256)} %param.19) | copy-start | bytes 3076
  107.4 2.3 copy-start.18
  107.4 2.3 copy-start.19
  107.4 2.1 copy-start.7
  107.4 2.1 copy-start.8
  107.4 3.0 copy-start.10
  109.5 1.4 copy-start.13
  109.7 0.7 copy-start.5
  109.7 1.2 copy-start.2
  112.8 83.4 %reduce-scatter.6.cloned.1.call-start = ((), (), s32[]{:S(2)}) async-start(), calls=%async_computation.7 | async-start | bytes 2621440 | tf_op jit(solution)/shard_map/reduce_scatter | solution.py:120
  162.1 34.1 %copy-start.4 = (bf16[8,64,256]{2,1,0:T(8,128)(2,1)S(1)}, bf16[8,64,256]{2,1,0:T(8,128)(2,1)}, u32[]{:S(2)}) copy-start(bf16[8,64,256]{2,1,0:T(8,128)(2,1)} %fusion.46) | copy-start | bytes 786436
  198.8 14.4 %all-to-all-start = ((bf16[8,64,256]{2,1,0:T(8,128)(2,1)}), bf16[8,64,256]{2,1,0:T(8,128)(2,1)S(1)}, u32[]{:S(2)}, u32[]{:S(2)}) async-start(bf16[8,64,256]{2,1,0:T(8,128)(2,1)} %bitcast.70), calls=%async_computation.1 | async-start | bytes 524288 | tf_op jit(solution)/shard_map/all_to_all | solution.py:154
  204.3 99.5 %reduce-scatter.8.cloned.1.call-start = ((), (), s32[]{:S(2)}) async-start(), calls=%async_computation.10 | async-start | bytes 4718592 | tf_op jit(solution)/shard_map/reduce_scatter | solution.py:171
  217.1 0.7 copy-start.21
  217.1 154.1 %reduce-scatter.14.cloned.1.call-start = ((), (), s32[]{:S(2)}) async-start(), calls=%async_computation.13 | async-start | bytes 1179648 | tf_op jit(solution)/shard_map/reduce_scatter | solution.py:174
  220.7 2.6 copy-start.3
  220.7 217.0 %reduce-scatter.10.cloned.1.call-start = ((), (), s32[]{:S(2)}) async-start(), calls=%async_computation.11 | async-start | bytes 1179648 | tf_op jit(solution)/shard_map/reduce_scatter | solution.py:172
  223.2 281.4 %reduce-scatter.12.cloned.1.call-start = ((), (), s32[]{:S(2)}) async-start(), calls=%async_computation.12 | async-start | bytes 1179648 | tf_op jit(solution)/shard_map/reduce_scatter | solution.py:173
Sparse Core Ops, SparseCore 0:
  35.9 19.4 all-gather.2
  56.9 16.8 all-gather.4
  112.9 49.1 all-reduce.5
  164.6 31.4 reduce-scatter.5
  217.2 86.5 reduce-scatter.7
  308.0 63.1 reduce-scatter.13
  375.2 62.4 reduce-scatter.9
  442.1 62.4 reduce-scatter.11
